TPU v7x, 1024 devices: a whole 8x8x8 slice. The times are simulated.
1024 devices in a mesh: grp: 16 (over y, core), aa: 64 (over x, z).
Axes of the slice: x: 8, y: 8, z: 8, core: 2. Of those that a mesh axis runs over, the one named last changes fastest.
Arguments:
- spectrum: float32 [1600, 2048, 128], P(None, ('grp', 'aa')), may hold values from 0.05 to 2
- friction: float32 [2048, 128], P(('grp', 'aa')), may hold values from 0.2 to 1
- wind_dir: float32 [2048, 128], P(('grp', 'aa')), may hold values from -3.140625 to 3.140625
- wet: int32 [2048, 128], P('grp'), may hold values 0 or 1
- owner: int32 [262144, 1], P(('grp', 'aa')), may hold values from 0 to 15; in each aligned block of 256 rows (0 to 255, 256 to 511, ...) at most 32 rows name the same one
- cell: int32 [2048, 128], P(('grp', 'aa')), may hold values from 0 to 255
Outputs:
- new_spectrum: float32 [1600, 2048, 128], P(None, ('grp', 'aa'))
- forcing: float32 [3, 262144], P(None, ('grp', 'aa'))
Inputs may be any that keep to these rules, and one draw needn't show every extreme that they name: Among the 256 points of one device no owner is named more than 32 times; some owner is named exactly 32 times.
All inputs are finite; a program needn't handle non-finite values. No bound on the sum of `wet` on one device may be relied on, other than what follows from the above.
Results may differ from a plain program's by a relative error of at most 0.0001.
Values sent between devices are 32-bit elements; how exact they have to be, the bound alone decides.
A program may use at most 32 MiB of HBM per device.

v0:
```python
import math

import jax
import jax.numpy as jnp
from jax import lax
from jax.sharding import PartitionSpec as P

FREQS = 50
DIRS = 32
ITERS = 2
OC_TILE = 256


COURANT = 0.7


def padded_2(cells, sides, width):
    for axis, dim in sides:
        count = lax.axis_size(axis)
        ends = count - 1
        head = lax.slice_in_dim(cells, 0, width, axis=dim)
        tail = lax.slice_in_dim(cells, cells.shape[dim] - width, cells.shape[dim], axis=dim)
        cells = jnp.concatenate(
            [
                lax.ppermute(tail, axis, [(i, (i + 1) % count) for i in range(ends)]),
                cells,
                lax.ppermute(head, axis, [((i + 1) % count, i) for i in range(ends)]),
            ],
            axis=dim,
        )
    return cells


def spectral_tables(count):
    index = jnp.arange(count, dtype=jnp.int32)
    freq_index = (index // DIRS).astype(jnp.float32)
    dir_index = (index % DIRS).astype(jnp.float32)
    relative = freq_index / jnp.float32(max(FREQS - 1, 1))
    angle = jnp.float32(2.0 * math.pi) * dir_index / jnp.float32(DIRS)
    speed = jnp.power(jnp.float32(0.5), relative)
    return (relative, angle, speed)


def source_terms(spectrum, total, friction, wind_dir, wetness, relative, angle):
    growth = (
        0.4
        * friction[None]
        * (0.5 + relative)[:, None, None]
        * jnp.maximum(jnp.cos(angle[:, None, None] - wind_dir[None]), 0.0)
    )
    damping = 0.6 * (0.25 + relative)[:, None, None] * (total / (1.0 + total))[None]
    return wetness[None] * spectrum * jnp.exp(growth - damping)


def advect(padded, courant_x, courant_y):
    center = padded[:, 1:-1]
    south = padded[:, :-2]
    north = padded[:, 2:]
    side = jnp.pad(center, ((0, 0), (0, 0), (1, 1)))
    west = side[:, :, :-2]
    east = side[:, :, 2:]
    speed_x = courant_x[:, None, None]
    speed_y = courant_y[:, None, None]
    return (
        center
        - jnp.maximum(speed_x, 0.0) * (center - west)
        - jnp.minimum(speed_x, 0.0) * (east - center)
        - jnp.maximum(speed_y, 0.0) * (center - south)
        - jnp.minimum(speed_y, 0.0) * (north - center)
    )


def stress_weights(angle, count):
    cosine = jnp.cos(angle)
    sine = jnp.sin(angle)
    return jnp.stack([0.5 * cosine * cosine, 0.5 * cosine * sine, 0.5 * sine * sine]) / jnp.float32(
        count
    )


def on_device(spectrum, friction, wind_dir, wet, owner, cell):
    count = spectrum.shape[0]
    rows_here = spectrum.shape[1]
    columns = spectrum.shape[2]
    aa_index = lax.axis_index("aa")
    group_wet = wet.astype(jnp.float32)
    own_wet = lax.dynamic_slice_in_dim(group_wet, aa_index * rows_here, rows_here, 0)
    relative, angle, speed = spectral_tables(count)
    total = jnp.mean(spectrum, axis=0)
    energy = source_terms(spectrum, total, friction, wind_dir, own_wet, relative, angle)
    width = count // lax.axis_size("aa")
    ang_part = lax.dynamic_slice_in_dim(angle, aa_index * width, width, 0)
    spd_part = lax.dynamic_slice_in_dim(speed, aa_index * width, width, 0)
    courant_x = COURANT * spd_part * jnp.cos(ang_part)
    courant_y = COURANT * spd_part * jnp.sin(ang_part)
    components = lax.all_to_all(energy, "aa", split_axis=0, concat_axis=1, tiled=True)
    for substep in range(ITERS):
        padded = padded_2(components, (("grp", 1),), 1)
        components = group_wet[None] * advect(padded, courant_x, courant_y)
    energy = lax.all_to_all(components, "aa", split_axis=1, concat_axis=0, tiled=True)
    weights = stress_weights(angle, count)
    stress = jnp.dot(weights, energy.reshape(count, -1), precision=lax.Precision.HIGHEST)
    groups = lax.axis_size("grp")
    points = rows_here * columns
    capacity = 2 * points // groups
    owners = owner[:, 0]
    onehot = (owners[:, None] == jnp.arange(groups, dtype=jnp.int32)[None]).astype(jnp.int32)
    before = jnp.cumsum(onehot, axis=0) - onehot
    ranking = jnp.sum(before * onehot, axis=1)
    target = owners * capacity + ranking
    buffer = jnp.zeros((3, groups * capacity), jnp.float32).at[:, target].set(stress)
    labels = jnp.full((1, groups * capacity), -1, jnp.int32).at[0, target].set(cell.reshape(-1))
    got_values, got_labels = (
        lax.all_to_all(buffer, "grp", split_axis=1, concat_axis=1, tiled=True),
        lax.all_to_all(labels, "grp", split_axis=1, concat_axis=1, tiled=True),
    )
    table = (got_labels[0][:, None] == jnp.arange(OC_TILE, dtype=jnp.int32)[None]).astype(
        jnp.float32
    )
    forcing = jnp.dot(got_values, table, precision=lax.Precision.HIGHEST)
    return (energy, forcing)


def solution(mesh):
    placed = (
        P(None, ("grp", "aa"), None),
        P(("grp", "aa"), None),
        P(("grp", "aa"), None),
        P("grp", None),
        P(("grp", "aa"), None),
        P(("grp", "aa"), None),
    )
    return jax.shard_map(
        on_device,
        mesh=mesh,
        in_specs=placed,
        out_specs=(P(None, ("grp", "aa"), None), P(None, ("grp", "aa"))),
        check_vma=False,
    )
```

profile of v0, /device:TPU:13, one launch (start us, length us, event | category | flops | bytes accessed | tf_op | source)
XLA Modules:
  0.0 213.5 jit_solution(12576825378404324718)
XLA Ops:
  0.7 1.0 convert_element_type.58
  1.7 3.0 %reduce_sum.20 = f32[2,128]{1,0:T(2,128)S(1)} reduce(f32[1600,2,128]{2,1,0:T(2,128)} %param.6, f32[]{:T(128)} %constant.86.clone.1), dimensions={0}, to_apply=%region_0.1 | reduce | flops 409344 | bytes 1639428 | tf_op jit(solution)/shard_map/reduce_sum | solution.py:89
  4.7 25.3 %exponential_multiply_fusion = f32[1600,2,128]{2,1,0:T(2,128)} fusion(f32[1600,2,128]{2,1,0:T(2,128)S(1)} %copy-done, f32[2,128]{1,0:T(2,128)S(1)} %get-tuple-element.14, f32[2,128]{1,0:T(2,128)S(1)} %copy-done.3, f32[2,128]{1,0:T(2,128)S(1)} %get-tuple-element.15, f32[2,128]{1,0:T(2,128)S(1)} %constant_dynamic-slice_fusion, f32[1600]{0:T(1024)S(1)} %get-tuple-element.13, ...), kind=kLoop, calls=%fused_computation.39 | loop fusion | flops 3276800 | bytes 3300096 | tf_op jit(solution)/shard_map/mul | solution.py:52
  30.0 22.2 %all-to-all-start = ((f32[1600,2,128]{2,1,0:T(2,128)}), f32[1600,2,128]{2,1,0:T(2,128)S(1)}, u32[]{:S(2)}, u32[]{:S(2)}) async-start(f32[1600,2,128]{2,1,0:T(2,128)} %exponential_multiply_fusion), calls=%async_computation | async-start | bytes 3276800 | tf_op jit(solution)/shard_map/all_to_all | solution.py:96
  52.3 40.1 %all-to-all-done = f32[1600,2,128]{2,1,0:T(2,128)S(1)} async-done(((f32[1600,2,128]{2,1,0:T(2,128)}), f32[1600,2,128]{2,1,0:T(2,128)S(1)}, u32[]{:S(2)}, u32[]{:S(2)}) %all-to-all-start) | async-done | bytes 1638432 | tf_op jit(solution)/shard_map/all_to_all | solution.py:96
  93.3 5.5 %collective-permute-start = (f32[25,1,128]{2,1,0:T(1,128)S(1)}, f32[25,1,128]{2,1,0:T(1,128)S(1)}, u32[]{:S(2)}, u32[]{:S(2)}) collective-permute-start(f32[25,1,128]{2,1,0:T(1,128)S(1)} %get-tuple-element.8), channel_id=1, source_target_pairs={{0,64},{64,128},{128,192},{192,256},{256,320},{320,384},{384,448},... | collective-permute-start | bytes 38408 | tf_op jit(solution)/shard_map/ppermute | solution.py:25
  98.8 1.9 collective-permute-start.1
  100.8 3.1 %collective-permute-done.1 = f32[25,1,128]{2,1,0:T(1,128)S(1)} collective-permute-done((f32[25,1,128]{2,1,0:T(1,128)S(1)}, f32[25,1,128]{2,1,0:T(1,128)S(1)}, u32[]{:S(2)}, u32[]{:S(2)}) %collective-permute-start.1) | collective-permute-done | bytes 12832 | tf_op jit(solution)/shard_map/ppermute | solution.py:27
  103.8 2.0 fusion.6
  105.8 1.9 collective-permute-start.2
  107.8 2.4 %collective-permute-start.3 = (f32[25,1,128]{2,1,0:T(1,128)S(1)}, f32[25,1,128]{2,1,0:T(1,128)S(1)}, u32[]{:S(2)}, u32[]{:S(2)}) collective-permute-start(f32[25,1,128]{2,1,0:T(1,128)S(1)} %get-tuple-element.7), channel_id=1, source_target_pairs={{64,0},{128,64},{192,128},{256,192},{320,256},{384,320},{448,384},... | collective-permute-start | bytes 38408 | tf_op jit(solution)/shard_map/ppermute | solution.py:27
  110.2 2.7 %collective-permute-done.3 = f32[25,1,128]{2,1,0:T(1,128)S(1)} collective-permute-done((f32[25,1,128]{2,1,0:T(1,128)S(1)}, f32[25,1,128]{2,1,0:T(1,128)S(1)}, u32[]{:S(2)}, u32[]{:S(2)}) %collective-permute-start.3) | collective-permute-done | bytes 12832 | tf_op jit(solution)/shard_map/ppermute | solution.py:27
  112.9 2.0 fusion.15
  114.8 2.3 %copy.26 = f32[25,128,128]{2,0,1:T(8,128)} copy(f32[25,128,128]{2,1,0:T(8,128)S(1)} %fusion.15) | data formatting | bytes 3276800 | tf_op jit(solution)/shard_map/mul | solution.py:99
  117.2 9.1 %all-to-all-start.1 = ((f32[25,128,128]{2,0,1:T(8,128)}), f32[25,128,128]{2,0,1:T(8,128)S(1)}, u32[]{:S(2)}, u32[]{:S(2)}) async-start(f32[25,128,128]{2,0,1:T(8,128)} %copy.26), calls=%async_computation.1 | async-start | bytes 4194304 | tf_op jit(solution)/shard_map/all_to_all | solution.py:100
  127.3 1.6 scatter_custom_fusion.1
  129.9 48.5 %all-to-all-done.1 = f32[25,128,128]{2,0,1:T(8,128)S(1)} async-done(((f32[25,128,128]{2,0,1:T(8,128)}), f32[25,128,128]{2,0,1:T(8,128)S(1)}, u32[]{:S(2)}, u32[]{:S(2)}) %all-to-all-start.1) | async-done | bytes 1638432 | tf_op jit(solution)/shard_map/all_to_all | solution.py:100
  178.5 13.0 %all-to-all-start.3 = ((s32[1,16,32]{2,0,1:T(1,128)}), s32[1,16,32]{2,0,1:T(1,128)S(1)}, u32[]{:S(2)}, u32[]{:S(2)}) async-start(s32[1,16,32]{2,0,1:T(1,128)} %all_to_all.51), calls=%async_computation.3 | async-start | bytes 16384 | tf_op jit(solution)/shard_map/all_to_all | solution.py:115
  191.5 1.0 copy.27
  193.0 2.8 %fusion.18 = f32[256,3]{1,0:T(8,128)S(1)} fusion(f32[200,8,2,128]{3,2,1,0:T(2,128)S(1)} %bitcast.43, f32[1,1600]{1,0:T(1,128)S(1)} %get-tuple-element.16, f32[1,1600]{1,0:T(1,128)S(1)} %get-tuple-element.17, f32[1,1600]{1,0:T(1,128)S(1)} %multiply_multiply_fusion.2), kind=kOutput, calls=%fused_computation.24 | convolution fusion | flops 14760000 | bytes 1660672 | tf_op jit(solution)/shard_map/dot_general | solution.py:102
  195.8 1.2 scatter_custom_fusion
  198.5 6.6 %all-to-all-start.2 = ((f32[3,16,32]{2,0,1:T(4,128)}), f32[3,16,32]{2,0,1:T(4,128)S(1)}, u32[]{:S(2)}, u32[]{:S(2)}) async-start(f32[3,16,32]{2,0,1:T(4,128)} %copy.32), calls=%async_computation.2 | async-start | bytes 65536 | tf_op jit(solution)/shard_map/all_to_all | solution.py:114
  206.3 6.1 %all-to-all-done.2 = f32[3,16,32]{2,0,1:T(4,128)S(1)} async-done(((f32[3,16,32]{2,0,1:T(4,128)}), f32[3,16,32]{2,0,1:T(4,128)S(1)}, u32[]{:S(2)}, u32[]{:S(2)}) %all-to-all-start.2) | async-done | bytes 6176 | tf_op jit(solution)/shard_map/all_to_all | solution.py:114
  212.5 0.9 fusion.29
  (41 shorter events, 6.5 us)
Async XLA Ops:
  0.6 4.0 %copy-start = (f32[1600,2,128]{2,1,0:T(2,128)S(1)}, f32[1600,2,128]{2,1,0:T(2,128)}, u32[]{:S(2)}) copy-start(f32[1600,2,128]{2,1,0:T(2,128)} %param.6) | copy-start | bytes 4915204
  0.6 4.0 %copy-start.4 = (f32[2,128]{1,0:T(2,128)S(1)}, f32[2,128]{1,0:T(2,128)}, u32[]{:S(2)}) copy-start(f32[2,128]{1,0:T(2,128)} %param.7) | copy-start | bytes 3076
  0.7 4.0 %copy-start.3 = (f32[2,128]{1,0:T(2,128)S(1)}, f32[2,128]{1,0:T(2,128)}, u32[]{:S(2)}) copy-start(f32[2,128]{1,0:T(2,128)} %param.8) | copy-start | bytes 3076
  30.0 62.5 %all-to-all-start = ((f32[1600,2,128]{2,1,0:T(2,128)}), f32[1600,2,128]{2,1,0:T(2,128)S(1)}, u32[]{:S(2)}, u32[]{:S(2)}) async-start(f32[1600,2,128]{2,1,0:T(2,128)} %exponential_multiply_fusion), calls=%async_computation | async-start | bytes 3276800 | tf_op jit(solution)/shard_map/all_to_all | solution.py:96
  93.3 7.4 %collective-permute-start = (f32[25,1,128]{2,1,0:T(1,128)S(1)}, f32[25,1,128]{2,1,0:T(1,128)S(1)}, u32[]{:S(2)}, u32[]{:S(2)}) collective-permute-start(f32[25,1,128]{2,1,0:T(1,128)S(1)} %get-tuple-element.8), channel_id=1, source_target_pairs={{0,64},{64,128},{128,192},{192,256},{256,320},{320,384},{384,448},... | collective-permute-start | bytes 38408 | tf_op jit(solution)/shard_map/ppermute | solution.py:25
  98.8 5.0 %collective-permute-start.1 = (f32[25,1,128]{2,1,0:T(1,128)S(1)}, f32[25,1,128]{2,1,0:T(1,128)S(1)}, u32[]{:S(2)}, u32[]{:S(2)}) collective-permute-start(f32[25,1,128]{2,1,0:T(1,128)S(1)} %get-tuple-element.9), channel_id=1, source_target_pairs={{64,0},{128,64},{192,128},{256,192},{320,256},{384,320},{448,384},... | collective-permute-start | bytes 38408 | tf_op jit(solution)/shard_map/ppermute | solution.py:27
  105.8 4.3 %collective-permute-start.2 = (f32[25,1,128]{2,1,0:T(1,128)S(1)}, f32[25,1,128]{2,1,0:T(1,128)S(1)}, u32[]{:S(2)}, u32[]{:S(2)}) collective-permute-start(f32[25,1,128]{2,1,0:T(1,128)S(1)} %get-tuple-element.6), channel_id=1, source_target_pairs={{0,64},{64,128},{128,192},{192,256},{256,320},{320,384},{384,448},... | collective-permute-start | bytes 38408 | tf_op jit(solution)/shard_map/ppermute | solution.py:25
  107.8 5.1 %collective-permute-start.3 = (f32[25,1,128]{2,1,0:T(1,128)S(1)}, f32[25,1,128]{2,1,0:T(1,128)S(1)}, u32[]{:S(2)}, u32[]{:S(2)}) collective-permute-start(f32[25,1,128]{2,1,0:T(1,128)S(1)} %get-tuple-element.7), channel_id=1, source_target_pairs={{64,0},{128,64},{192,128},{256,192},{320,256},{384,320},{448,384},... | collective-permute-start | bytes 38408 | tf_op jit(solution)/shard_map/ppermute | solution.py:27
  117.2 9.2 %copy-start.2 = (s32[256,1]{0,1:T(1,128)S(1)}, s32[256,1]{0,1:T(1,128)}, u32[]{:S(2)}) copy-start(s32[256,1]{0,1:T(1,128)} %param.10) | copy-start | bytes 3076
  117.2 61.3 %all-to-all-start.1 = ((f32[25,128,128]{2,0,1:T(8,128)}), f32[25,128,128]{2,0,1:T(8,128)S(1)}, u32[]{:S(2)}, u32[]{:S(2)}) async-start(f32[25,128,128]{2,0,1:T(8,128)} %copy.26), calls=%async_computation.1 | async-start | bytes 4194304 | tf_op jit(solution)/shard_map/all_to_all | solution.py:100
  178.5 20.0 %all-to-all-start.3 = ((s32[1,16,32]{2,0,1:T(1,128)}), s32[1,16,32]{2,0,1:T(1,128)S(1)}, u32[]{:S(2)}, u32[]{:S(2)}) async-start(s32[1,16,32]{2,0,1:T(1,128)} %all_to_all.51), calls=%async_computation.3 | async-start | bytes 16384 | tf_op jit(solution)/shard_map/all_to_all | solution.py:115
  193.0 20.5 %copy-start.1 = (f32[64,25,2,128]{3,2,1,0:T(2,128)}, f32[64,25,2,128]{3,2,1,0:T(2,128)S(1)}, u32[]{:S(2)}) copy-start(f32[64,25,2,128]{3,2,1,0:T(2,128)S(1)} %copy.28) | copy-start | bytes 4915204
  198.5 14.0 %all-to-all-start.2 = ((f32[3,16,32]{2,0,1:T(4,128)}), f32[3,16,32]{2,0,1:T(4,128)S(1)}, u32[]{:S(2)}, u32[]{:S(2)}) async-start(f32[3,16,32]{2,0,1:T(4,128)} %copy.32), calls=%async_computation.2 | async-start | bytes 65536 | tf_op jit(solution)/shard_map/all_to_all | solution.py:114
where the time goes:
time: 214 us; the launch traced here: 213 us
  waiting for transfers between devices  101 us (47%)
  starting transfers between devices  62.6 us (29%)
  other arithmetic  35.1 us (16%)
  local copies, waits for them, and re-layouts  9.87 us (5%)
  matrix products  3.76 us (2%)
    all_to_all x1, waiting for transfers between devices, on_device(): lax.all_to_all(components, 'aa', split_axis=1, concat_axis=0, tiled=True)  48.5 us
    all_to_all x1, waiting for transfers between devices, on_device(): lax.all_to_all(energy, 'aa', split_axis=0, concat_axis=1, tiled=True)  40.1 us
    mul x1, other arithmetic, source_terms(): return wetness[None] * spectrum * jnp.exp(growth - damping)  25.3 us
    all_to_all x1, starting transfers between devices, on_device(): lax.all_to_all(energy, 'aa', split_axis=0, concat_axis=1, tiled=True)  22.2 us
    all_to_all x1, starting transfers between devices, on_device(): lax.all_to_all(labels, 'grp', split_axis=1, concat_axis=1, tiled=True)  13 us
    all_to_all x1, starting transfers between devices, on_device(): lax.all_to_all(components, 'aa', split_axis=1, concat_axis=0, tiled=True)  9.14 us
    ppermute x2, starting transfers between devices, padded_2(): lax.ppermute(tail, axis, [(i, (i + 1) % count) for i in range(ends)])  7.39 us
    all_to_all x1, starting transfers between devices, on_device(): lax.all_to_all(buffer, 'grp', split_axis=1, concat_axis=1, tiled=True)  6.56 us
  transfers between devices with their start and end apart: 8, of which 6 were waited for; matrix products, arithmetic and copies ran while one was open for 5% of the time, Pallas kernels for 0%

commit v1 on v0

v1 whole, which is shorter than its diff:
```python
import functools
import math

import jax
import jax.numpy as jnp
from jax import lax
from jax.experimental import pallas as pl
from jax.experimental.pallas import tpu as pltpu
from jax.sharding import PartitionSpec as P

MESH = pl.DeviceIdType.MESH
DIRS = 32
COURANT = 0.7
LOG2E = math.log2(math.e)
CHUNK = 2
WINDOW = 25
LOADS = 5
F32 = jnp.float32

EDGE = (1, 1, 0, 0)
WEST = (True, False, False, True)


def row(ref, index):
    return ref[pl.ds(index, 1), :]


def roll_up(cells, west):
    return pltpu.roll(cells, 1 if west else 127, 1)


def kernel(
    freqs,
    spectrum_hbm,
    friction_hbm,
    wind_hbm,
    wet_hbm,
    owner_hbm,
    cell_hbm,
    out_hbm,
    forcing_ref,
    spectrum,
    friction,
    wind,
    wet,
    owner,
    cell,
    stepped,
    send_up,
    send_down,
    got_up,
    got_down,
    inner,
    coefs,
    scales,
    moments,
    edge_send,
    edge_got,
    parts,
    parts_got,
    load_sem,
    small_sem,
    up_send_sem,
    up_recv_sem,
    down_send_sem,
    down_recv_sem,
    edge_send_sem,
    edge_recv_sem,
    part_send_sem,
    part_recv_sem,
    out_sem,
):
    groups, column = lax.axis_size("grp"), lax.axis_size("aa")
    my_grp, my_aa = lax.axis_index("grp"), lax.axis_index("aa")
    devices = groups * column
    me = my_grp * column + my_aa
    after = lax.rem(me + 1, devices)
    before = lax.rem(me + devices - 1, devices)
    next_id = (after // column, lax.rem(after, column))
    prev_id = (before // column, lax.rem(before, column))
    chunks = freqs // CHUNK
    rows_all = spectrum.shape[0]
    piece = rows_all // LOADS

    loads = [
        pltpu.make_async_copy(
            spectrum_hbm.at[pl.ds(i * piece, piece)], spectrum.at[pl.ds(i * piece, piece)], load_sem.at[i]
        )
        for i in range(LOADS)
    ]
    wet_start = pl.multiple_of((2 * my_aa) // 8 * 8, 8)
    smalls = [
        pltpu.make_async_copy(friction_hbm, friction, small_sem.at[0]),
        pltpu.make_async_copy(wind_hbm, wind, small_sem.at[1]),
        pltpu.make_async_copy(wet_hbm.at[pl.ds(wet_start, 8)], wet, small_sem.at[2]),
        pltpu.make_async_copy(owner_hbm, owner, small_sem.at[3]),
        pltpu.make_async_copy(cell_hbm, cell, small_sem.at[4]),
    ]
    for copy in smalls[:3] + loads + smalls[3:]:
        copy.start()
    barrier = pltpu.get_barrier_semaphore()
    for neighbour in (next_id, prev_id):
        pl.semaphore_signal(barrier, inc=1, device_id=neighbour, device_id_type=MESH)
    for turn in range(1, groups):
        peer = lax.rem(my_grp + turn, groups)
        pl.semaphore_signal(barrier, inc=1, device_id=(peer, my_aa), device_id_type=MESH)

    lane = lax.broadcasted_iota(jnp.int32, (8, 128), 1)
    turn8 = lax.broadcasted_iota(jnp.int32, (8, 128), 0)
    cos0 = jnp.full((8, 128), 1.0, F32)
    sin0 = jnp.full((8, 128), 0.0, F32)
    for j in range(1, 8):
        cos0 = jnp.where(turn8 == j, F32(math.cos(2.0 * math.pi * j / DIRS)), cos0)
        sin0 = jnp.where(turn8 == j, F32(math.sin(2.0 * math.pi * j / DIRS)), sin0)
    cosine = (cos0, -sin0, -cos0, sin0)
    sine = (sin0, cos0, -sin0, -cos0)
    abs_x = [COURANT * c for c in (cos0, sin0, cos0, sin0)]
    abs_y = [COURANT * c for c in (sin0, cos0, sin0, cos0)]
    speed_sum = COURANT * (cos0 + sin0)
    side = [jnp.where(lane != 0, 1.0, 0.0) if west else jnp.where(lane != 127, 1.0, 0.0) for west in WEST]

    number = lax.broadcasted_iota(jnp.int32, scales.shape[1:], 0).astype(F32) * F32(1.0 / max(freqs - 1, 1))
    scales[0] = number
    scales[1] = jnp.exp2(-number)
    moments[...] = jnp.zeros_like(moments)
    edge_send[...] = jnp.zeros_like(edge_send)

    for copy in smalls[:3]:
        copy.wait()
    has = [jnp.where(me > 0, 1.0, 0.0).astype(F32), jnp.where(me < devices - 1, 1.0, 0.0).astype(F32)]
    wet_row = lax.rem(2 * my_aa, 8)
    wetness = [jnp.broadcast_to(row(wet, wet_row + y).astype(F32), (8, 128)) for y in range(2)]
    wind_cos, wind_sin = jnp.cos(wind[...]), jnp.sin(wind[...])
    grow = [
        [
            0.4
            * friction[y : y + 1, :]
            * jnp.maximum(cosine[g] * wind_cos[y : y + 1, :] + sine[g] * wind_sin[y : y + 1, :], 0.0)
            for y in range(2)
        ]
        for g in range(4)
    ]

    acc = jnp.zeros((8, 128), F32)
    for i in range(LOADS):
        loads[i].wait()
        tiles = piece // 64

        def add(t, acc, i=i):
            at = pl.multiple_of(i * piece + t * 64, 64)
            return acc + jnp.sum(spectrum[pl.ds(at, 64), :].reshape(8, 8, 128), axis=0)

        acc = lax.fori_loop(0, tiles, add, acc, unroll=2)
    parity = lax.rem(turn8, 2)
    total = [
        jnp.sum(jnp.where(parity == y, acc, 0.0), axis=0, keepdims=True) / F32(rows_all // 2) for y in range(2)
    ]
    damp = [t / (1.0 + t) for t in total]

    for g in range(4):
        for y in range(2):
            coefs[0, g * 2 + y] = LOG2E * (0.5 * grow[g][y] - 0.15 * damp[y])
            coefs[1, g * 2 + y] = LOG2E * (grow[g][y] - 0.6 * damp[y])
            coefs[2, g * 2 + y] = wetness[y] * side[g] * abs_x[g]
            pull = wetness[y] * abs_y[g]
            if y != EDGE[g]:
                pull = pull * (has[0] if g < 2 else has[1])
            coefs[3, g * 2 + y] = pull
    coefs[4, 0] = wetness[0]
    coefs[4, 1] = wetness[1]
    coefs[4, 2] = speed_sum

    def scale(index, k):
        return jnp.broadcast_to(scales[index, pl.ds(k, 1), :], (8, 128))

    def slope(g, y, cells, other):
        pulled = coefs[2, g * 2 + y] * roll_up(cells, WEST[g])
        if other is not None:
            pulled = pulled + coefs[3, g * 2 + y] * other
        return coefs[4, 2] * cells - pulled

    pl.semaphore_wait(barrier, groups + 1)

    def copies(c):
        return (
            pltpu.make_async_remote_copy(
                src_ref=send_up.at[c],
                dst_ref=got_up.at[c],
                send_sem=up_send_sem.at[c],
                recv_sem=up_recv_sem.at[c],
                device_id=next_id,
                device_id_type=MESH,
            ),
            pltpu.make_async_remote_copy(
                src_ref=send_down.at[c],
                dst_ref=got_down.at[c],
                send_sem=down_send_sem.at[c],
                recv_sem=down_recv_sem.at[c],
                device_id=prev_id,
                device_id_type=MESH,
            ),
        )

    def start(c):
        for copy in copies(c):
            copy.start()

    def make(c, carry):
        for g in range(4):
            e = EDGE[g]
            o = 1 - e
            sums = [[moments[g * 6 + y * 3 + m] for m in range(3)] for y in range(2)]
            for kk in range(CHUNK):
                k = c * CHUNK + kk
                base = k * 64 + g * 16
                q, s = scale(0, k), scale(1, k)
                energy = []
                for y in range(2):
                    cells = spectrum[pl.ds(base + y, 8, stride=2), :]
                    power = jnp.exp2(coefs[0, g * 2 + y] + q * coefs[1, g * 2 + y])
                    energy.append(coefs[4, y] * cells * power)
                    first = s * energy[y]
                    sums[y][0] = sums[y][0] + energy[y]
                    sums[y][1] = sums[y][1] + first
                    sums[y][2] = sums[y][2] + s * first
                step = energy[e] - s * slope(g, e, energy[e], energy[o])
                send = send_up if g < 2 else send_down
                at = (kk * 2 + g % 2) * 16
                send[c, pl.ds(at, 8), :] = energy[e]
                send[c, pl.ds(at + 8, 8), :] = step
                inner[c, pl.ds((kk * 4 + g) * 8, 8), :] = energy[o]
            for y in range(2):
                for m in range(3):
                    moments[g * 6 + y * 3 + m] = sums[y][m]

        @pl.when(c < WINDOW)
        def _():
            start(c)

        return carry

    lax.fori_loop(0, chunks, make, 0)

    def weigh(g):
        per = F32(1.0 / (rows_all // 2))
        return (
            0.5 * per * cosine[g] * cosine[g],
            0.5 * per * cosine[g] * sine[g],
            0.5 * per * sine[g] * sine[g],
        )

    def reduce8(cells):
        return jnp.sum(cells, axis=0, keepdims=True)

    own = [[jnp.zeros((8, 128), F32) for _ in range(2)] for _ in range(3)]
    for d in range(2):
        direct = [jnp.zeros((8, 128), F32) for _ in range(3)]
        double = [jnp.zeros((8, 128), F32) for _ in range(3)]
        for gi in range(2):
            g = 2 * d + gi
            e = EDGE[g]
            o = 1 - e
            m_e = [moments[g * 6 + e * 3 + m] for m in range(3)]
            m_o = [moments[g * 6 + o * 3 + m] for m in range(3)]
            slope_o2 = slope(g, o, m_o[2], None)
            slope_e2 = slope(g, e, m_e[2], m_o[2])
            sum_o = m_o[0] - 2.0 * slope(g, o, m_o[1], None) + slope(g, o, slope_o2, None)
            sum_e = m_e[0] - 2.0 * slope(g, e, m_e[1], m_o[1]) + slope(g, e, slope_e2, slope_o2)
            weights = weigh(g)
            reach = abs_y[g] * (2.0 * m_e[1] - speed_sum * m_e[2] - slope_e2)
            sideways = abs_x[g] * abs_y[g] * m_e[2]
            twice = abs_y[g] * abs_y[g] * m_e[2]
            for i in range(3):
                own[i][e] = own[i][e] + weights[i] * sum_e
                own[i][o] = own[i][o] + weights[i] * sum_o
                direct[i] = direct[i] + weights[i] * reach
                double[i] = double[i] + weights[i] * twice
                edge_send[d, 8 + gi * 3 + i : 9 + gi * 3 + i, :] = reduce8(weights[i] * sideways)
        for i in range(3):
            edge_send[d, i : i + 1, :] = reduce8(direct[i])
            edge_send[d, 3 + i : 4 + i, :] = reduce8(double[i])
    edges = [
        pltpu.make_async_remote_copy(
            src_ref=edge_send.at[d],
            dst_ref=edge_got.at[d],
            send_sem=edge_send_sem.at[d],
            recv_sem=edge_recv_sem.at[d],
            device_id=next_id if d == 0 else prev_id,
            device_id_type=MESH,
        )
        for d in range(2)
    ]
    for copy in edges:
        copy.start()
    stress = [[reduce8(own[i][y]) for y in range(2)] for i in range(3)]

    def finish(c, carry):
        @pl.when(c + WINDOW < chunks)
        def _():
            start(c + WINDOW)

        for copy in copies(c):
            copy.wait_recv()
        for kk in range(CHUNK):
            for g in range(4):
                e = EDGE[g]
                o = 1 - e
                k = c * CHUNK + kk
                s = scale(1, k)
                send = send_up if g < 2 else send_down
                got = got_up if g < 2 else got_down
                at = (kk * 2 + g % 2) * 16
                start_o = inner[c, pl.ds((kk * 4 + g) * 8, 8), :]
                one_e = send[c, pl.ds(at + 8, 8), :]
                one_o = start_o - s * slope(g, o, start_o, got[c, pl.ds(at, 8), :])
                two_o = one_o - s * slope(g, o, one_o, got[c, pl.ds(at + 8, 8), :])
                two_e = one_e - s * slope(g, e, one_e, one_o)
                base = k * 64 + g * 16
                stepped[pl.ds(base + o, 8, stride=2), :] = two_o
                stepped[pl.ds(base + e, 8, stride=2), :] = two_e
        put(c).start()
        return carry

    def put(c):
        at = pl.multiple_of(c * (CHUNK * 64), 64)
        return pltpu.make_async_copy(
            stepped.at[pl.ds(at, CHUNK * 64)], out_hbm.at[pl.ds(at, CHUNK * 64)], out_sem.at[c]
        )

    first_stop, second_stop = chunks // 4, (3 * chunks) // 4
    lax.fori_loop(0, first_stop, finish, 0)

    for copy in edges:
        copy.wait_recv()
    for copy in smalls[3:]:
        copy.wait()
    for d in range(2):
        o, e = d, 1 - d
        here = has[d] * coefs[4, o][:1]
        both = here * coefs[4, e][:1]
        sideways = edge_got[d, 8:16, :] * coefs[4, o]
        for i in range(3):
            moved = edge_got[d, i : i + 1, :]
            for gi in range(2):
                g = 2 * d + gi
                moved = moved + (side[g] * roll_up(sideways, WEST[g]))[gi * 3 + i : gi * 3 + i + 1]
            stress[i][o] = stress[i][o] + here * moved
            stress[i][e] = stress[i][e] + both * edge_got[d, 3 + i : 4 + i, :]

    target = lax.broadcasted_iota(jnp.int32, (groups * 8, 128), 0)
    place = lax.broadcasted_iota(jnp.int32, (128, 128), 0)
    summed = jnp.zeros((groups * 8, 128), F32)
    for y in range(2):
        cells = cell[y : y + 1, :]
        high = jnp.where(cells >= 128, 1, 0)
        goal = owner[y : y + 1, :] * 8 + high * 3
        spread = jnp.zeros((groups * 8, 128), F32)
        for i in range(3):
            spread = jnp.where(target == goal + i, stress[i][y], spread)
        table = jnp.where(place == cells - high * 128, 1.0, 0.0).astype(F32)
        summed = summed + lax.dot_general(
            spread,
            table,
            (((1,), (1,)), ((), ())),
            precision=lax.Precision.HIGHEST,
            preferred_element_type=F32,
        )
    parts[...] = summed.reshape(groups, 8, 128)

    def part(turn):
        peer = lax.rem(my_grp + turn, groups)
        return pltpu.make_async_remote_copy(
            src_ref=parts.at[peer],
            dst_ref=parts_got.at[turn],
            send_sem=part_send_sem.at[turn],
            recv_sem=part_recv_sem.at[turn],
            device_id=(peer, my_aa),
            device_id_type=MESH,
        )

    for turn in range(1, groups):
        part(turn).start()

    lax.fori_loop(first_stop, second_stop, finish, 0)

    forcing = parts[my_grp]
    for turn in range(1, groups):
        part(turn).wait_recv()
        forcing = forcing + parts_got[turn]
    forcing_ref[:, 0:128] = forcing[0:3]
    forcing_ref[:, 128:256] = forcing[3:6]

    lax.fori_loop(second_stop, chunks, finish, 0)

    for turn in range(1, groups):
        part(turn).wait_send()
    for copy in edges:
        copy.wait_send()

    def drain(c, carry):
        for copy in copies(c):
            copy.wait_send()
        put(c).wait()
        return carry

    lax.fori_loop(0, chunks, drain, 0)


def on_device(groups, spectrum, friction, wind_dir, wet, owner, cell):
    comps, rows, width = spectrum.shape
    freqs = comps // DIRS
    chunks = freqs // CHUNK
    any_space = pl.BlockSpec(memory_space=pl.ANY)
    dma = pltpu.SemaphoreType.DMA
    new, forcing = pl.pallas_call(
        functools.partial(kernel, freqs),
        out_shape=(
            jax.ShapeDtypeStruct((comps * rows, width), F32),
            jax.ShapeDtypeStruct((3, 256), F32),
        ),
        in_specs=[any_space] * 6,
        out_specs=(any_space, pl.BlockSpec(memory_space=pltpu.VMEM)),
        scratch_shapes=[
            pltpu.VMEM((comps * rows, width), F32),
            pltpu.VMEM((rows, width), F32),
            pltpu.VMEM((rows, width), F32),
            pltpu.VMEM((8, width), jnp.int32),
            pltpu.VMEM((rows, width), jnp.int32),
            pltpu.VMEM((rows, width), jnp.int32),
            pltpu.VMEM((comps * rows, width), F32),
            pltpu.VMEM((chunks, CHUNK * 32, width), F32),
            pltpu.VMEM((chunks, CHUNK * 32, width), F32),
            pltpu.VMEM((chunks, CHUNK * 32, width), F32),
            pltpu.VMEM((chunks, CHUNK * 32, width), F32),
            pltpu.VMEM((chunks, CHUNK * 32, width), F32),
            pltpu.VMEM((5, 8, 8, width), F32),
            pltpu.VMEM((2, (freqs + 7) // 8 * 8, width), F32),
            pltpu.VMEM((24, 8, width), F32),
            pltpu.VMEM((2, 16, width), F32),
            pltpu.VMEM((2, 16, width), F32),
            pltpu.VMEM((groups, 8, width), F32),
            pltpu.VMEM((groups, 8, width), F32),
            dma((LOADS,)),
            dma((5,)),
            dma((chunks,)),
            dma((chunks,)),
            dma((chunks,)),
            dma((chunks,)),
            dma((2,)),
            dma((2,)),
            dma((groups,)),
            dma((groups,)),
            dma((chunks,)),
        ],
        compiler_params=pltpu.CompilerParams(
            collective_id=0, has_side_effects=True, vmem_limit_bytes=60 * 1024 * 1024
        ),
    )(
        spectrum.reshape(comps * rows, width),
        friction,
        wind_dir,
        wet,
        owner.reshape(rows, width),
        cell,
    )
    return new.reshape(comps, rows, width), forcing


def solution(mesh):
    placed = (
        P(None, ("grp", "aa"), None),
        P(("grp", "aa"), None),
        P(("grp", "aa"), None),
        P("grp", None),
        P(("grp", "aa"), None),
        P(("grp", "aa"), None),
    )
    return jax.shard_map(
        functools.partial(on_device, mesh.shape["grp"]),
        mesh=mesh,
        in_specs=placed,
        out_specs=(P(None, ("grp", "aa"), None), P(None, ("grp", "aa"))),
        check_vma=False,
    )
```

time: 214 us -> 57.9 us (0.27)
  the two profiles are of different devices: /device:TPU:13 before, /device:TPU:1 now
where the time goes in v1:
time: 57.9 us; the launch traced here: 57.7 us
  Pallas kernels  54.1 us (93%)
  local copies, waits for them, and re-layouts  2.96 us (5%)
  between operations  0.65 us (1%)
    pallas_call x1, Pallas kernels, on_device(): pl.pallas_call(functools.partial(kernel, freqs), out_shape=(jax.ShapeDtyp...  54.1 us
    unnamed x4, local copies, waits for them, and re-layouts  2.96 us

profile of v1, /device:TPU:1, one launch (start us, length us, event | category | flops | bytes accessed | tf_op | source)
XLA Modules:
  0.0 57.7 jit_solution(16276019858264994742)
XLA Ops:
  0.6 54.1 %shard_map.77 = (f32[3200,128]{1,0:T(8,128)}, f32[3,256]{1,0:T(4,128)}) custom-call(f32[3200,128]{1,0:T(8,128)} %bitcast.4, f32[2,128]{1,0:T(2,128)} %friction_hbm.1, f32[2,128]{1,0:T(2,128)} %wind_hbm.1, s32[128,128]{1,0:T(8,128)} %wet_hbm.1, s32[2,128]{1,0:T(2,128)} %bitcast.5, s32[2,128]{1,0:T(2,128)} %cell_hbm.1), custom_call_target="tpu_custom_call" | custom-call | tf_op jit(solution)/shard_map/pallas_call | solution.py:415
  54.8 0.0 copy-start
  54.8 2.4 %copy.10 = f32[1600,2,128]{2,1,0:T(2,128)} copy(f32[1600,2,128]{2,1,0:T(2,128)} %bitcast.3) | data formatting | bytes 3276800
  57.1 0.0 copy-done
  57.1 0.6 %copy.11 = f32[3,256]{1,0:T(4,128)} copy(f32[3,256]{1,0:T(4,128)S(1)} %copy-done) | data formatting | bytes 6144
Async XLA Ops:
  54.8 2.4 %copy-start = (f32[3,256]{1,0:T(4,128)S(1)}, f32[3,256]{1,0:T(4,128)}, u32[]{:S(2)}) copy-start(f32[3,256]{1,0:T(4,128)} %get-tuple-element.9) | copy-start | bytes 9220

commit v2 on v1

v2 whole, which is shorter than its diff:
```python
import functools
import math

import jax
import jax.numpy as jnp
from jax import lax
from jax.experimental import pallas as pl
from jax.experimental.pallas import tpu as pltpu
from jax.sharding import PartitionSpec as P

MESH = pl.DeviceIdType.MESH
DIRS = 32
COURANT = 0.7
LOG2E = math.log2(math.e)
CHUNKS = (0, 15, 24, 33, 41, 47, 50)
FIRST, SECOND = 1, 3
PIECES = 4
LIMIT = 60 * 1024 * 1024
F32 = jnp.float32

EDGE = (1, 1, 0, 0)
WEST = (True, False, False, True)


def roll_up(cells, west):
    return pltpu.roll(cells, 1 if west else 127, 1)


def wide(cells):
    return jnp.broadcast_to(cells, (8, 128))


def reduce8(cells):
    return jnp.sum(cells, axis=0, keepdims=True)


def kernel(
    chunks,
    spectrum_hbm,
    friction_hbm,
    wind_hbm,
    wet_hbm,
    owner_hbm,
    cell_hbm,
    out_hbm,
    forcing_hbm,
    spectrum,
    friction,
    wind,
    wet,
    owner,
    cell,
    stepped,
    got,
    near,
    far,
    mine,
    others,
    coefs,
    halo,
    scales,
    moments,
    edge_send,
    edge_got,
    parts,
    parts_got,
    forcing,
    load_sem,
    small_sem,
    send_sem,
    recv_sem,
    tile_send_sem,
    tile_recv_sem,
    edge_send_sem,
    edge_recv_sem,
    part_send_sem,
    part_recv_sem,
    out_sem,
    forcing_sem,
    here_sem,
    all_sem,
):
    freqs = spectrum.shape[0]
    groups, column = lax.axis_size("grp"), lax.axis_size("aa")
    my_grp, my_aa = lax.axis_index("grp"), lax.axis_index("aa")
    devices = groups * column
    me = my_grp * column + my_aa
    after = lax.rem(me + 1, devices)
    before = lax.rem(me + devices - 1, devices)
    row_ids = ((after // column, lax.rem(after, column)), (before // column, lax.rem(before, column)))
    last = len(chunks) - 1

    barrier = pltpu.get_barrier_semaphore()
    for other in row_ids:
        pl.semaphore_signal(barrier, inc=1, device_id=other, device_id_type=MESH)

    @pl.when(my_grp == 0)
    def _():
        for peer in range(1, groups):
            pl.semaphore_signal(barrier, inc=1, device_id=(peer, my_aa), device_id_type=MESH)

    half = freqs // 2
    loads = [
        pltpu.make_async_copy(spectrum_hbm.at[pl.ds(i * half, half)], spectrum.at[pl.ds(i * half, half)], load_sem.at[i])
        for i in range(2)
    ]
    wet_start = pl.multiple_of((2 * my_aa) // 8 * 8, 8)
    smalls = [
        pltpu.make_async_copy(friction_hbm, friction, small_sem.at[0]),
        pltpu.make_async_copy(wind_hbm, wind, small_sem.at[1]),
        pltpu.make_async_copy(wet_hbm.at[pl.ds(wet_start, 8)], wet, small_sem.at[2]),
        pltpu.make_async_copy(owner_hbm, owner, small_sem.at[3]),
        pltpu.make_async_copy(cell_hbm, cell, small_sem.at[4]),
    ]
    for copy in smalls[:3] + loads + smalls[3:]:
        copy.start()
    pl.semaphore_wait(barrier, jnp.where(my_grp == 0, 2, 3))

    def bulk(d, c):
        where = pl.ds(chunks[c], chunks[c + 1] - chunks[c])
        return pltpu.make_async_remote_copy(
            src_ref=spectrum_hbm.at[where, pl.ds(32 * d, 32)],
            dst_ref=got.at[d, where],
            send_sem=send_sem.at[d],
            recv_sem=recv_sem.at[d, c],
            device_id=row_ids[d],
            device_id_type=MESH,
        )

    for d in range(2):
        bulk(d, 0).start()

    @pl.when(my_grp != 0)
    def _():
        pl.semaphore_signal(here_sem, inc=1, device_id=(0, my_aa), device_id_type=MESH)

    lane = lax.broadcasted_iota(jnp.int32, (8, 128), 1)
    place8 = lax.broadcasted_iota(jnp.int32, (8, 128), 0)
    cos0 = jnp.full((8, 128), 1.0, F32)
    sin0 = jnp.full((8, 128), 0.0, F32)
    for j in range(1, 8):
        cos0 = jnp.where(place8 == j, F32(math.cos(2.0 * math.pi * j / DIRS)), cos0)
        sin0 = jnp.where(place8 == j, F32(math.sin(2.0 * math.pi * j / DIRS)), sin0)
    cosine = (cos0, -sin0, -cos0, sin0)
    sine = (sin0, cos0, -sin0, -cos0)
    abs_x = [COURANT * c for c in (cos0, sin0, cos0, sin0)]
    abs_y = [COURANT * c for c in (sin0, cos0, sin0, cos0)]
    speed_sum = COURANT * (cos0 + sin0)
    side = [jnp.where(lane != 0, 1.0, 0.0) if west else jnp.where(lane != 127, 1.0, 0.0) for west in WEST]
    number = lax.broadcasted_iota(jnp.int32, scales.shape[1:], 0).astype(F32) * F32(1.0 / max(freqs - 1, 1))
    scales[0] = number
    scales[1] = jnp.exp2(-number)
    edge_send[...] = jnp.zeros_like(edge_send)
    has = [jnp.where(me > 0, 1.0, 0.0).astype(F32), jnp.where(me < devices - 1, 1.0, 0.0).astype(F32)]

    for copy in smalls[:3]:
        copy.wait()
    grow = 0.4 * friction[...]
    mine[0:2, :] = grow * jnp.cos(wind[...])
    mine[2:4, :] = grow * jnp.sin(wind[...])
    wet_row = lax.rem(2 * my_aa, 8)
    for y in range(2):
        mine[6 + y : 7 + y, :] = wet[pl.ds(wet_row + y, 1), :].astype(F32)

    def add(k, acc):
        return acc + jnp.sum(spectrum[k].reshape(8, 8, 128), axis=0)

    acc = jnp.zeros((8, 128), F32)
    for i in range(2):
        loads[i].wait()
        acc = lax.fori_loop(i * half, (i + 1) * half, add, acc)
    for y in range(2):
        total = reduce8(jnp.where(lax.rem(place8, 2) == y, acc, 0.0)) / F32(freqs * DIRS)
        mine[4 + y : 5 + y, :] = total / (1.0 + total)

    def tile(d):
        return pltpu.make_async_remote_copy(
            src_ref=mine,
            dst_ref=others.at[d],
            send_sem=tile_send_sem.at[d],
            recv_sem=tile_recv_sem.at[d],
            device_id=row_ids[d],
            device_id_type=MESH,
        )

    for d in range(2):
        tile(d).start()

    def exponent(values, g, y):
        growth = jnp.maximum(cosine[g] * values[0 + y : 1 + y] + sine[g] * values[2 + y : 3 + y], 0.0)
        damp = values[4 + y : 5 + y]
        return LOG2E * (0.5 * growth - 0.15 * damp), LOG2E * (growth - 0.6 * damp)

    values = mine[...]
    for g in range(4):
        for y in range(2):
            coefs[0, g * 2 + y], coefs[1, g * 2 + y] = exponent(values, g, y)
            coefs[2, g * 2 + y] = values[6 + y : 7 + y] * side[g] * abs_x[g]
            pull = values[6 + y : 7 + y] * abs_y[g]
            coefs[3, g * 2 + y] = pull if y == EDGE[g] else pull * has[g // 2]
    for y in range(2):
        coefs[4, y] = wide(values[6 + y : 7 + y])
    coefs[4, 2] = speed_sum

    def scale(index, k):
        return wide(scales[index, pl.ds(k, 1), :])

    def slope(g, y, cells, other):
        pulled = coefs[2, g * 2 + y] * roll_up(cells, WEST[g])
        if other is not None:
            pulled = pulled + coefs[3, g * 2 + y] * other
        return coefs[4, 2] * cells - pulled

    for d in range(2):

        def make(k, sums, d=d):
            q, s = scale(0, k), scale(1, k)
            new = []
            for gi in range(2):
                g = 2 * d + gi
                e = EDGE[g]
                energy = []
                for y in range(2):
                    cells = spectrum[k, pl.ds(g * 16 + y, 8, stride=2), :]
                    power = jnp.exp2(coefs[0, g * 2 + y] + q * coefs[1, g * 2 + y])
                    energy.append(coefs[4, y] * cells * power)
                    first = s * energy[y]
                    old = sums[(gi * 2 + y) * 3 : (gi * 2 + y) * 3 + 3]
                    new += [old[0] + energy[y], old[1] + first, old[2] + s * first]
                near[k, g] = energy[1 - e]
                far[k, g] = energy[e] - s * slope(g, e, energy[e], energy[1 - e])
            return tuple(new)

        sums = lax.fori_loop(0, freqs, make, (jnp.zeros((8, 128), F32),) * 12)
        for i in range(12):
            moments[d * 12 + i] = sums[i]

    def weigh(g):
        per = F32(1.0 / (freqs * DIRS))
        return (
            0.5 * per * cosine[g] * cosine[g],
            0.5 * per * cosine[g] * sine[g],
            0.5 * per * sine[g] * sine[g],
        )

    own = [[jnp.zeros((8, 128), F32) for _ in range(2)] for _ in range(3)]
    for d in range(2):
        direct = [jnp.zeros((8, 128), F32) for _ in range(3)]
        double = [jnp.zeros((8, 128), F32) for _ in range(3)]
        for gi in range(2):
            g = 2 * d + gi
            e = EDGE[g]
            o = 1 - e
            m_e = [moments[g * 6 + e * 3 + m] for m in range(3)]
            m_o = [moments[g * 6 + o * 3 + m] for m in range(3)]
            slope_o2 = slope(g, o, m_o[2], None)
            slope_e2 = slope(g, e, m_e[2], m_o[2])
            sum_o = m_o[0] - 2.0 * slope(g, o, m_o[1], None) + slope(g, o, slope_o2, None)
            sum_e = m_e[0] - 2.0 * slope(g, e, m_e[1], m_o[1]) + slope(g, e, slope_e2, slope_o2)
            weights = weigh(g)
            reach = abs_y[g] * (2.0 * m_e[1] - speed_sum * m_e[2] - slope_e2)
            sideways = abs_x[g] * abs_y[g] * m_e[2]
            twice = abs_y[g] * abs_y[g] * m_e[2]
            for i in range(3):
                own[i][e] = own[i][e] + weights[i] * sum_e
                own[i][o] = own[i][o] + weights[i] * sum_o
                direct[i] = direct[i] + weights[i] * reach
                double[i] = double[i] + weights[i] * twice
                edge_send[d, 8 + gi * 3 + i : 9 + gi * 3 + i, :] = reduce8(weights[i] * sideways)
        for i in range(3):
            edge_send[d, i : i + 1, :] = reduce8(direct[i])
            edge_send[d, 3 + i : 4 + i, :] = reduce8(double[i])

    def edge(d):
        return pltpu.make_async_remote_copy(
            src_ref=edge_send.at[d],
            dst_ref=edge_got.at[d],
            send_sem=edge_send_sem.at[d],
            recv_sem=edge_recv_sem.at[d],
            device_id=row_ids[d],
            device_id_type=MESH,
        )

    for d in range(2):
        edge(d).start()
    for c in range(1, last):
        for d in range(2):
            bulk(d, c).start()

    @pl.when(my_grp == 0)
    def _():
        pl.semaphore_wait(here_sem, groups - 1)
        for peer in range(1, groups):
            pl.semaphore_signal(all_sem, inc=1, device_id=(peer, my_aa), device_id_type=MESH)

    stress = [[reduce8(own[i][y]) for y in range(2)] for i in range(3)]

    for d in range(2):
        tile(d).wait_recv()
        values = others[d]
        for g in (2 * d, 2 * d + 1):
            e = EDGE[g]
            for y in range(2):
                halo[0, g * 2 + y], halo[1, g * 2 + y] = exponent(values, g, y)
            halo[2, g] = values[6 + e : 7 + e] * side[g] * abs_x[g]
            halo[3, g] = values[6 + e : 7 + e] * abs_y[g]
        for y in range(2):
            halo[4, d * 2 + y] = wide(values[6 + y : 7 + y])

    def finish(k, carry):
        q, s = scale(0, k), scale(1, k)
        for g in range(4):
            d, e = g // 2, EDGE[g]
            o = 1 - e
            base = (g % 2) * 16
            there = []
            for y in range(2):
                cells = got[d, k, pl.ds(base + y, 8, stride=2), :]
                power = jnp.exp2(halo[0, g * 2 + y] + q * halo[1, g * 2 + y])
                there.append(halo[4, d * 2 + y] * cells * power)
            pulled = halo[2, g] * roll_up(there[e], WEST[g]) + halo[3, g] * there[o]
            there_one = there[e] - s * (coefs[4, 2] * there[e] - pulled)
            start_o = near[k, g]
            one_e = far[k, g]
            one_o = start_o - s * slope(g, o, start_o, there[e])
            two_o = one_o - s * slope(g, o, one_o, there_one)
            two_e = one_e - s * slope(g, e, one_e, one_o)
            stepped[k, pl.ds(g * 16 + o, 8, stride=2), :] = two_o
            stepped[k, pl.ds(g * 16 + e, 8, stride=2), :] = two_e
        return carry

    def put(start, stop):
        where = pl.ds(start, stop - start)
        return pltpu.make_async_copy(stepped.at[where], out_hbm.at[where], out_sem)

    def finish_chunk(c):
        for d in range(2):
            bulk(d, c).wait_recv()
        lax.fori_loop(chunks[c], chunks[c + 1], finish, 0)
        put(chunks[c], chunks[c + 1]).start()

    for c in range(FIRST):
        finish_chunk(c)

    for d in range(2):
        edge(d).wait_recv()
    for copy in smalls[3:]:
        copy.wait()
    for d in range(2):
        o, e = d, 1 - d
        here = has[d] * coefs[4, o][:1]
        both = here * coefs[4, e][:1]
        sideways = edge_got[d, 8:16, :] * coefs[4, o]
        for i in range(3):
            moved = edge_got[d, i : i + 1, :]
            for gi in range(2):
                g = 2 * d + gi
                moved = moved + (side[g] * roll_up(sideways, WEST[g]))[gi * 3 + i : gi * 3 + i + 1]
            stress[i][o] = stress[i][o] + here * moved
            stress[i][e] = stress[i][e] + both * edge_got[d, 3 + i : 4 + i, :]

    target = lax.broadcasted_iota(jnp.int32, (groups * 8, 128), 0)
    place = lax.broadcasted_iota(jnp.int32, (128, 128), 0)
    summed = jnp.zeros((groups * 8, 128), F32)
    for y in range(2):
        cells = cell[y : y + 1, :]
        high = jnp.where(cells >= 128, 1, 0)
        goal = owner[y : y + 1, :] * 8 + high * 3
        spread = jnp.zeros((groups * 8, 128), F32)
        for i in range(3):
            spread = jnp.where(target == goal + i, stress[i][y], spread)
        table = jnp.where(place == cells - high * 128, 1.0, 0.0).astype(F32)
        summed = summed + lax.dot_general(
            spread,
            table,
            (((1,), (1,)), ((), ())),
            precision=lax.Precision.HIGHEST,
            preferred_element_type=F32,
        )
    parts[...] = summed.reshape(groups, 8, 128)

    @pl.when(my_grp != 0)
    def _():
        pl.semaphore_wait(all_sem, 1)

    for turn in range(1, groups):
        peer = lax.rem(my_grp + turn, groups)
        pltpu.make_async_remote_copy(
            src_ref=parts.at[peer],
            dst_ref=parts_got.at[turn - 1],
            send_sem=part_send_sem,
            recv_sem=part_recv_sem,
            device_id=(peer, my_aa),
            device_id_type=MESH,
        ).start()

    for c in range(FIRST, SECOND):
        finish_chunk(c)

    pltpu.make_async_copy(parts_got, parts_got, part_recv_sem).wait()
    summed = parts[my_grp]
    for turn in range(1, groups):
        summed = summed + parts_got[turn - 1]
    forcing[:, 0:128] = summed[0:3]
    forcing[:, 128:256] = summed[3:6]
    forcing_copy = pltpu.make_async_copy(forcing, forcing_hbm, forcing_sem)
    forcing_copy.start()

    for c in range(SECOND, last):
        finish_chunk(c)

    pltpu.make_async_copy(parts_got, parts_got, part_send_sem).wait()
    for d in range(2):
        tile(d).wait_send()
        edge(d).wait_send()
        pltpu.make_async_copy(got.at[d], got.at[d], send_sem.at[d]).wait()
    forcing_copy.wait()
    put(0, freqs).wait()


def pass_on(new, forcing, new_out, forcing_out, held, held_forcing, in_sem, out_sem):
    step = -(-held.shape[0] // PIECES)
    pairs = []
    for i in range(PIECES):
        where = pl.ds(i * step, min(step, held.shape[0] - i * step))
        pairs.append((new.at[where], held.at[where], new_out.at[where]))
    pairs.append((forcing, held_forcing, forcing_out))
    loads = [pltpu.make_async_copy(src, mid, in_sem.at[i]) for i, (src, mid, _) in enumerate(pairs)]
    stores = [pltpu.make_async_copy(mid, dst, out_sem.at[i]) for i, (_, mid, dst) in enumerate(pairs)]
    for copy in loads:
        copy.start()
    for load, store in zip(loads, stores):
        load.wait()
        store.start()
    for copy in stores:
        copy.wait()


def on_device(groups, spectrum, friction, wind_dir, wet, owner, cell):
    comps, rows, width = spectrum.shape
    freqs = comps // DIRS
    chunks = CHUNKS if CHUNKS[-1] == freqs else tuple(range(0, freqs + 1, 2))
    last = len(chunks) - 1
    anywhere = pl.BlockSpec(memory_space=pl.ANY)
    dma = pltpu.SemaphoreType.DMA
    results = (
        jax.ShapeDtypeStruct((freqs, 2 * DIRS, width), F32),
        jax.ShapeDtypeStruct((3, 256), F32),
    )
    vmem = pltpu.VMEM
    new, forcing = pl.pallas_call(
        functools.partial(kernel, chunks),
        out_shape=results,
        in_specs=[anywhere] * 6,
        out_specs=(anywhere, anywhere),
        scratch_shapes=[
            vmem((freqs, 2 * DIRS, width), F32),
            vmem((rows, width), F32),
            vmem((rows, width), F32),
            vmem((8, width), jnp.int32),
            vmem((rows, width), jnp.int32),
            vmem((rows, width), jnp.int32),
            vmem((freqs, 2 * DIRS, width), F32),
            vmem((2, freqs, DIRS, width), F32),
            vmem((freqs, 4, 8, width), F32),
            vmem((freqs, 4, 8, width), F32),
            vmem((8, width), F32),
            vmem((2, 8, width), F32),
            vmem((5, 8, 8, width), F32),
            vmem((5, 8, 8, width), F32),
            vmem((2, (freqs + 7) // 8 * 8, width), F32),
            vmem((24, 8, width), F32),
            vmem((2, 16, width), F32),
            vmem((2, 16, width), F32),
            vmem((groups, 8, width), F32),
            vmem((groups - 1, 8, width), F32),
            vmem((3, 256), F32),
            dma((2,)),
            dma((5,)),
            dma((2,)),
            dma((2, last)),
            dma((2,)),
            dma((2,)),
            dma((2,)),
            dma((2,)),
            dma,
            dma,
            dma,
            dma,
            pltpu.SemaphoreType.REGULAR,
            pltpu.SemaphoreType.REGULAR,
        ],
        compiler_params=pltpu.CompilerParams(
            collective_id=0, has_side_effects=True, vmem_limit_bytes=LIMIT
        ),
    )(
        spectrum.reshape(freqs, 2 * DIRS, width),
        friction,
        wind_dir,
        wet,
        owner.reshape(rows, width),
        cell,
    )
    new, forcing = pl.pallas_call(
        pass_on,
        out_shape=results,
        in_specs=[anywhere] * 2,
        out_specs=(anywhere, anywhere),
        scratch_shapes=[
            vmem((freqs, 2 * DIRS, width), F32),
            vmem((3, 256), F32),
            dma((PIECES + 1,)),
            dma((PIECES + 1,)),
        ],
        compiler_params=pltpu.CompilerParams(vmem_limit_bytes=LIMIT),
    )(new, forcing)
    return new.reshape(comps, rows, width), forcing


def solution(mesh):
    placed = (
        P(None, ("grp", "aa"), None),
        P(("grp", "aa"), None),
        P(("grp", "aa"), None),
        P("grp", None),
        P(("grp", "aa"), None),
        P(("grp", "aa"), None),
    )
    return jax.shard_map(
        functools.partial(on_device, mesh.shape["grp"]),
        mesh=mesh,
        in_specs=placed,
        out_specs=(P(None, ("grp", "aa"), None), P(None, ("grp", "aa"))),
        check_vma=False,
    )
```

time: 57.9 us -> 48.4 us (0.84)
  Pallas kernels: 54.1 us -> 47.6 us
  local copies, waits for them, and re-layouts: 2.96 us -> 0 us
    pallas_call x1 -> x2, Pallas kernels: 54.1 us -> 47.6 us  [the longest x1 45.3 us: on_device(): pl.pallas_call(functools.partial(kernel, chunks), out_shape=results, in_s...]
    unnamed x4 -> x0, local copies, waits for them, and re-layouts: 2.96 us -> none
where the time goes in v2:
time: 48.4 us; the launch traced here: 48.2 us
  Pallas kernels  47.6 us (98%)
  between operations  0.64 us (1%)
    pallas_call x1, Pallas kernels, on_device(): pl.pallas_call(functools.partial(kernel, chunks), out_shape=results, in_s...  45.3 us
    pallas_call x1, Pallas kernels, on_device(): pl.pallas_call(pass_on, out_shape=results, in_specs=[anywhere] * 2, out_s...  2.25 us

profile of v2, /device:TPU:1, one launch (start us, length us, event | category | flops | bytes accessed | tf_op | source)
XLA Modules:
  0.0 48.2 jit_solution(9611414100031561539)
XLA Ops:
  0.6 45.3 %shard_map.77 = (f32[50,64,128]{2,1,0:T(8,128)}, f32[3,256]{1,0:T(4,128)}) custom-call(f32[50,64,128]{2,1,0:T(8,128)} %bitcast.3, f32[2,128]{1,0:T(2,128)} %friction_hbm.1, f32[2,128]{1,0:T(2,128)} %wind_hbm.1, s32[128,128]{1,0:T(8,128)} %wet_hbm.1, s32[2,128]{1,0:T(2,128)} %bitcast.4, s32[2,128]{1,0:T(2,128)} %cell_hbm.1), custom_call_target="tpu_custom_call" | custom-call | tf_op jit(solution)/shard_map/pallas_call | solution.py:451
  46.0 2.3 %shard_map.78 = (f32[50,64,128]{2,1,0:T(8,128)}, f32[3,256]{1,0:T(4,128)}) custom-call(f32[50,64,128]{2,1,0:T(8,128)} %get-tuple-element.6.new, f32[3,256]{1,0:T(4,128)} %get-tuple-element.7.forcing), custom_call_target="tpu_custom_call" | custom-call | tf_op jit(solution)/shard_map/pallas_call | solution.py:504

commit v3 on v2

--- a/solution.py
+++ b/solution.py
@@ -12,7 +12,7 @@
 DIRS = 32
 COURANT = 0.7
 LOG2E = math.log2(math.e)
-CHUNKS = (0, 15, 24, 33, 41, 47, 50)
+CHUNKS = (0, 15, 30, 45, 50)
 FIRST, SECOND = 1, 3
 PIECES = 4
 LIMIT = 60 * 1024 * 1024
@@ -231,7 +231,7 @@
                 far[k, g] = energy[e] - s * slope(g, e, energy[e], energy[1 - e])
             return tuple(new)
 
-        sums = lax.fori_loop(0, freqs, make, (jnp.zeros((8, 128), F32),) * 12)
+        sums = lax.fori_loop(0, freqs, make, (jnp.zeros((8, 128), F32),) * 12, unroll=10)
         for i in range(12):
             moments[d * 12 + i] = sums[i]
 
@@ -336,7 +336,7 @@
     def finish_chunk(c):
         for d in range(2):
             bulk(d, c).wait_recv()
-        lax.fori_loop(chunks[c], chunks[c + 1], finish, 0)
+        lax.fori_loop(chunks[c], chunks[c + 1], finish, 0, unroll=5)
         put(chunks[c], chunks[c + 1]).start()
 
     for c in range(FIRST):

time: 48.4 us -> 43.4 us (0.90)
  Pallas kernels: 47.6 us -> 42.6 us
    pallas_call x1, Pallas kernels: 45.3 us -> 40.4 us  [on_device(): pl.pallas_call(functools.partial(kernel, chunks), out_shape=results, in_s...]
where the time goes in v3:
time: 43.4 us; the launch traced here: 43.3 us
  Pallas kernels  42.6 us (98%)
  between operations  0.64 us (1%)
    pallas_call x1, Pallas kernels, on_device(): pl.pallas_call(functools.partial(kernel, chunks), out_shape=results, in_s...  40.4 us
    pallas_call x1, Pallas kernels, on_device(): pl.pallas_call(pass_on, out_shape=results, in_specs=[anywhere] * 2, out_s...  2.25 us

profile of v3, /device:TPU:1, one launch (start us, length us, event | category | flops | bytes accessed | tf_op | source)
XLA Modules:
  0.0 43.3 jit_solution(5641916923107780319)
XLA Ops:
  0.6 40.4 %shard_map.77 = (f32[50,64,128]{2,1,0:T(8,128)}, f32[3,256]{1,0:T(4,128)}) custom-call(f32[50,64,128]{2,1,0:T(8,128)} %bitcast.3, f32[2,128]{1,0:T(2,128)} %friction_hbm.1, f32[2,128]{1,0:T(2,128)} %wind_hbm.1, s32[128,128]{1,0:T(8,128)} %wet_hbm.1, s32[2,128]{1,0:T(2,128)} %bitcast.4, s32[2,128]{1,0:T(2,128)} %cell_hbm.1), custom_call_target="tpu_custom_call" | custom-call | tf_op jit(solution)/shard_map/pallas_call | solution.py:451
  41.0 2.3 %shard_map.78 = (f32[50,64,128]{2,1,0:T(8,128)}, f32[3,256]{1,0:T(4,128)}) custom-call(f32[50,64,128]{2,1,0:T(8,128)} %get-tuple-element.6.new, f32[3,256]{1,0:T(4,128)} %get-tuple-element.7.forcing), custom_call_target="tpu_custom_call" | custom-call | tf_op jit(solution)/shard_map/pallas_call | solution.py:504

commit v4 on v3

--- a/solution.py
+++ b/solution.py
@@ -12,13 +12,14 @@
 DIRS = 32
 COURANT = 0.7
 LOG2E = math.log2(math.e)
-CHUNKS = (0, 15, 30, 45, 50)
+CHUNKS = (0, 15, 30, 45, 48, 50)
 FIRST, SECOND = 1, 3
 PIECES = 4
 LIMIT = 60 * 1024 * 1024
 F32 = jnp.float32
 
 EDGE = (1, 1, 0, 0)
+SKIP = (2, 0)
 WEST = (True, False, False, True)
 
 
@@ -42,15 +43,14 @@
     wet_hbm,
     owner_hbm,
     cell_hbm,
-    out_hbm,
-    forcing_hbm,
+    stepped,
+    forcing,
     spectrum,
     friction,
     wind,
     wet,
     owner,
     cell,
-    stepped,
     got,
     near,
     far,
@@ -64,7 +64,6 @@
     edge_got,
     parts,
     parts_got,
-    forcing,
     load_sem,
     small_sem,
     send_sem,
@@ -75,8 +74,6 @@
     edge_recv_sem,
     part_send_sem,
     part_recv_sem,
-    out_sem,
-    forcing_sem,
     here_sem,
     all_sem,
 ):
@@ -91,6 +88,7 @@
     last = len(chunks) - 1
 
     barrier = pltpu.get_barrier_semaphore()
+    got[0, :, 0 : SKIP[0], :] = jnp.zeros((freqs, SKIP[0], 128), F32)
     for other in row_ids:
         pl.semaphore_signal(barrier, inc=1, device_id=other, device_id_type=MESH)
 
@@ -118,9 +116,10 @@
 
     def bulk(d, c):
         where = pl.ds(chunks[c], chunks[c + 1] - chunks[c])
+        first = SKIP[d]
         return pltpu.make_async_remote_copy(
-            src_ref=spectrum_hbm.at[where, pl.ds(32 * d, 32)],
-            dst_ref=got.at[d, where],
+            src_ref=spectrum_hbm.at[where, pl.ds(32 * d + first, 32 - first)],
+            dst_ref=got.at[d, where, pl.ds(first, 32 - first)],
             send_sem=send_sem.at[d],
             recv_sem=recv_sem.at[d, c],
             device_id=row_ids[d],
@@ -329,15 +328,10 @@
             stepped[k, pl.ds(g * 16 + e, 8, stride=2), :] = two_e
         return carry
 
-    def put(start, stop):
-        where = pl.ds(start, stop - start)
-        return pltpu.make_async_copy(stepped.at[where], out_hbm.at[where], out_sem)
-
     def finish_chunk(c):
         for d in range(2):
             bulk(d, c).wait_recv()
-        lax.fori_loop(chunks[c], chunks[c + 1], finish, 0, unroll=5)
-        put(chunks[c], chunks[c + 1]).start()
+        lax.fori_loop(chunks[c], chunks[c + 1], finish, 0, unroll=min(5, chunks[c + 1] - chunks[c]))
 
     for c in range(FIRST):
         finish_chunk(c)
@@ -403,8 +397,6 @@
         summed = summed + parts_got[turn - 1]
     forcing[:, 0:128] = summed[0:3]
     forcing[:, 128:256] = summed[3:6]
-    forcing_copy = pltpu.make_async_copy(forcing, forcing_hbm, forcing_sem)
-    forcing_copy.start()
 
     for c in range(SECOND, last):
         finish_chunk(c)
@@ -413,25 +405,19 @@
     for d in range(2):
         tile(d).wait_send()
         edge(d).wait_send()
-        pltpu.make_async_copy(got.at[d], got.at[d], send_sem.at[d]).wait()
-    forcing_copy.wait()
-    put(0, freqs).wait()
-
-
-def pass_on(new, forcing, new_out, forcing_out, held, held_forcing, in_sem, out_sem):
-    step = -(-held.shape[0] // PIECES)
-    pairs = []
+        whole = got.at[d, :, pl.ds(SKIP[d], 32 - SKIP[d])]
+        pltpu.make_async_copy(whole, whole, send_sem.at[d]).wait()
+
+
+def pass_on(new, forcing, new_out, forcing_out, sem):
+    step = -(-new.shape[0] // PIECES)
+    pairs = [(forcing, forcing_out)]
     for i in range(PIECES):
-        where = pl.ds(i * step, min(step, held.shape[0] - i * step))
-        pairs.append((new.at[where], held.at[where], new_out.at[where]))
-    pairs.append((forcing, held_forcing, forcing_out))
-    loads = [pltpu.make_async_copy(src, mid, in_sem.at[i]) for i, (src, mid, _) in enumerate(pairs)]
-    stores = [pltpu.make_async_copy(mid, dst, out_sem.at[i]) for i, (_, mid, dst) in enumerate(pairs)]
-    for copy in loads:
+        where = pl.ds(i * step, min(step, new.shape[0] - i * step))
+        pairs.append((new.at[where], new_out.at[where]))
+    stores = [pltpu.make_async_copy(src, dst, sem.at[i]) for i, (src, dst) in enumerate(pairs)]
+    for copy in stores:
         copy.start()
-    for load, store in zip(loads, stores):
-        load.wait()
-        store.start()
     for copy in stores:
         copy.wait()
 
@@ -448,11 +434,12 @@
         jax.ShapeDtypeStruct((3, 256), F32),
     )
     vmem = pltpu.VMEM
+    inside = pl.BlockSpec(memory_space=pltpu.VMEM)
     new, forcing = pl.pallas_call(
         functools.partial(kernel, chunks),
-        out_shape=results,
+        out_shape=(vmem((freqs, 2 * DIRS, width), F32), vmem((3, 256), F32)),
         in_specs=[anywhere] * 6,
-        out_specs=(anywhere, anywhere),
+        out_specs=(inside, inside),
         scratch_shapes=[
             vmem((freqs, 2 * DIRS, width), F32),
             vmem((rows, width), F32),
@@ -460,7 +447,6 @@
             vmem((8, width), jnp.int32),
             vmem((rows, width), jnp.int32),
             vmem((rows, width), jnp.int32),
-            vmem((freqs, 2 * DIRS, width), F32),
             vmem((2, freqs, DIRS, width), F32),
             vmem((freqs, 4, 8, width), F32),
             vmem((freqs, 4, 8, width), F32),
@@ -474,7 +460,6 @@
             vmem((2, 16, width), F32),
             vmem((groups, 8, width), F32),
             vmem((groups - 1, 8, width), F32),
-            vmem((3, 256), F32),
             dma((2,)),
             dma((5,)),
             dma((2,)),
@@ -483,8 +468,6 @@
             dma((2,)),
             dma((2,)),
             dma((2,)),
-            dma,
-            dma,
             dma,
             dma,
             pltpu.SemaphoreType.REGULAR,
@@ -504,15 +487,10 @@
     new, forcing = pl.pallas_call(
         pass_on,
         out_shape=results,
-        in_specs=[anywhere] * 2,
+        in_specs=[inside] * 2,
         out_specs=(anywhere, anywhere),
-        scratch_shapes=[
-            vmem((freqs, 2 * DIRS, width), F32),
-            vmem((3, 256), F32),
-            dma((PIECES + 1,)),
-            dma((PIECES + 1,)),
-        ],
-        compiler_params=pltpu.CompilerParams(vmem_limit_bytes=LIMIT),
+        scratch_shapes=[dma((PIECES + 1,))],
+        compiler_params=pltpu.CompilerParams(vmem_limit_bytes=4 * 1024 * 1024),
     )(new, forcing)
     return new.reshape(comps, rows, width), forcing
 

time: 43.4 us -> 40.6 us (0.935)
  Pallas kernels: 42.6 us -> 39.8 us
    pallas_call x2, Pallas kernels: 42.6 us -> 39.8 us  [the longest x1 38.6 us: on_device(): pl.pallas_call(functools.partial(kernel, chunks), out_shape=(vmem((freqs,...]
where the time goes in v4:
time: 40.6 us; the launch traced here: 40.5 us
  Pallas kernels  39.8 us (98%)
  between operations  0.64 us (2%)
    pallas_call x1, Pallas kernels, on_device(): pl.pallas_call(functools.partial(kernel, chunks), out_shape=(vmem((freqs,...  38.6 us
    pallas_call x1, Pallas kernels, on_device(): pl.pallas_call(pass_on, out_shape=results, in_specs=[inside] * 2, out_spe...  1.21 us

profile of v4, /device:TPU:1, one launch (start us, length us, event | category | flops | bytes accessed | tf_op | source)
XLA Modules:
  0.0 40.5 jit_solution(12453138032648498999)
XLA Ops:
  0.6 38.6 %shard_map.77 = (f32[50,64,128]{2,1,0:T(8,128)S(1)}, f32[3,256]{1,0:T(4,128)S(1)}) custom-call(f32[50,64,128]{2,1,0:T(8,128)} %bitcast.3, f32[2,128]{1,0:T(2,128)} %friction_hbm.1, f32[2,128]{1,0:T(2,128)} %wind_hbm.1, s32[128,128]{1,0:T(8,128)} %wet_hbm.1, s32[2,128]{1,0:T(2,128)} %bitcast.4, s32[2,128]{1,0:T(2,128)} %cell_hbm.1), custom_call_target="tpu_custom_call" | custom-call | tf_op jit(solution)/shard_map/pallas_call | solution.py:438
  39.2 1.2 %shard_map.78 = (f32[50,64,128]{2,1,0:T(8,128)}, f32[3,256]{1,0:T(4,128)}) custom-call(f32[50,64,128]{2,1,0:T(8,128)S(1)} %get-tuple-element.6.new, f32[3,256]{1,0:T(4,128)S(1)} %get-tuple-element.7.forcing), custom_call_target="tpu_custom_call" | custom-call | tf_op jit(solution)/shard_map/pallas_call | solution.py:487

commit v5 on v4

--- a/solution.py
+++ b/solution.py
@@ -12,7 +12,7 @@
 DIRS = 32
 COURANT = 0.7
 LOG2E = math.log2(math.e)
-CHUNKS = (0, 15, 30, 45, 48, 50)
+CHUNKS = (0, 15, 30, 44, 47, 50)
 FIRST, SECOND = 1, 3
 PIECES = 4
 LIMIT = 60 * 1024 * 1024
@@ -52,6 +52,7 @@
     owner,
     cell,
     got,
+    passing,
     near,
     far,
     mine,
@@ -74,6 +75,9 @@
     edge_recv_sem,
     part_send_sem,
     part_recv_sem,
+    pass_send_sem,
+    pass_recv_sem,
+    row_sem,
     here_sem,
     all_sem,
 ):
@@ -87,16 +91,49 @@
     row_ids = ((after // column, lax.rem(after, column)), (before // column, lax.rem(before, column)))
     last = len(chunks) - 1
 
+    line = 8 if column % 8 == 0 else column
+    place_in_line = lax.rem(my_aa, line)
+    is_first, is_last = place_in_line == 0, place_in_line == line - 1
+    is_inner = jnp.logical_and(place_in_line > 0, place_in_line < line - 1)
+    is_early = place_in_line < line - 2
+    is_late = place_in_line >= line - 2
+    ends = jnp.logical_or(is_first, is_last)
+
+    middle = line // 2
+    is_middle, is_low = place_in_line == middle, place_in_line == 1
+    ahead = lax.rem(me + line - 1, devices)
+    behind = lax.rem(me + devices - (line - 1), devices)
+    ahead_id = (ahead // column, lax.rem(ahead, column))
+    behind_id = (behind // column, lax.rem(behind, column))
+    to_middle, to_low = line - 1 - middle, middle - 1
     barrier = pltpu.get_barrier_semaphore()
-    got[0, :, 0 : SKIP[0], :] = jnp.zeros((freqs, SKIP[0], 128), F32)
-    for other in row_ids:
-        pl.semaphore_signal(barrier, inc=1, device_id=other, device_id_type=MESH)
+
+    @pl.when(ends)
+    def _():
+        pl.semaphore_signal(barrier, inc=1, device_id=row_ids[1], device_id_type=MESH)
+
+    @pl.when(is_early)
+    def _():
+        pl.semaphore_signal(barrier, inc=1, device_id=row_ids[0], device_id_type=MESH)
+
+    @pl.when(is_middle)
+    def _():
+        pl.semaphore_signal(barrier, inc=1, device_id=(my_grp, my_aa + to_middle), device_id_type=MESH)
+
+    @pl.when(is_low)
+    def _():
+        pl.semaphore_signal(barrier, inc=1, device_id=(my_grp, my_aa + to_low), device_id_type=MESH)
+
+    @pl.when(is_first)
+    def _():
+        pl.semaphore_signal(barrier, inc=1, device_id=behind_id, device_id_type=MESH)
 
     @pl.when(my_grp == 0)
     def _():
         for peer in range(1, groups):
             pl.semaphore_signal(barrier, inc=1, device_id=(peer, my_aa), device_id_type=MESH)
 
+    got[0, :, 0 : SKIP[0], :] = jnp.zeros((freqs, SKIP[0], 128), F32)
     half = freqs // 2
     loads = [
         pltpu.make_async_copy(spectrum_hbm.at[pl.ds(i * half, half)], spectrum.at[pl.ds(i * half, half)], load_sem.at[i])
@@ -110,9 +147,13 @@
         pltpu.make_async_copy(owner_hbm, owner, small_sem.at[3]),
         pltpu.make_async_copy(cell_hbm, cell, small_sem.at[4]),
     ]
-    for copy in smalls[:3] + loads + smalls[3:]:
-        copy.start()
-    pl.semaphore_wait(barrier, jnp.where(my_grp == 0, 2, 3))
+    rows_heard = jnp.where(is_first, 0, jnp.where(place_in_line == line - 2, 2, 1))
+    passes = jnp.logical_or(jnp.logical_or(is_middle, is_low), is_last)
+    heard = rows_heard + jnp.where(passes, 1, 0) + jnp.where(my_grp == 0, 0, 1)
+
+    @pl.when(heard > 0)
+    def _():
+        pl.semaphore_wait(barrier, heard)
 
     def bulk(d, c):
         where = pl.ds(chunks[c], chunks[c + 1] - chunks[c])
@@ -126,8 +167,46 @@
             device_id_type=MESH,
         )
 
-    for d in range(2):
-        bulk(d, 0).start()
+    block = pl.ds(chunks[last - 1], chunks[last] - chunks[last - 1])
+    lines = pl.ds(SKIP[0], 32 - SKIP[0])
+
+    def hop(source, target, other, sent, landed):
+        return pltpu.make_async_remote_copy(
+            src_ref=source, dst_ref=target, send_sem=sent, recv_sem=landed, device_id=other, device_id_type=MESH
+        )
+
+    passed = passing.at[:, lines]
+
+    @pl.when(is_late)
+    def _():
+        bulk(0, 0).start()
+
+    @pl.when(is_last)
+    def _():
+        hop(
+            spectrum_hbm.at[block, lines],
+            passed,
+            (my_grp, my_aa - to_middle),
+            send_sem.at[0],
+            pass_recv_sem,
+        ).start()
+
+    @pl.when(is_inner)
+    def _():
+        bulk(1, 0).start()
+        pl.semaphore_signal(row_sem.at[0], inc=1, device_id=row_ids[1], device_id_type=MESH)
+
+    @pl.when(is_late)
+    def _():
+        pl.semaphore_signal(row_sem.at[1], inc=1, device_id=row_ids[0], device_id_type=MESH)
+
+    for copy in smalls[:3] + loads + smalls[3:]:
+        copy.start()
+
+    @pl.when(is_early)
+    def _():
+        pl.semaphore_wait(row_sem.at[0], 1)
+        bulk(0, 0).start()
 
     @pl.when(my_grp != 0)
     def _():
@@ -182,8 +261,11 @@
             device_id_type=MESH,
         )
 
-    for d in range(2):
-        tile(d).start()
+    tile(0).start()
+
+    @pl.when(is_inner)
+    def _():
+        tile(1).start()
 
     def exponent(values, g, y):
         growth = jnp.maximum(cosine[g] * values[0 + y : 1 + y] + sine[g] * values[2 + y : 3 + y], 0.0)
@@ -280,11 +362,30 @@
             device_id_type=MESH,
         )
 
-    for d in range(2):
-        edge(d).start()
-    for c in range(1, last):
-        for d in range(2):
-            bulk(d, c).start()
+    edge(0).start()
+    for c in range(1, last - 1):
+        bulk(0, c).start()
+
+    @pl.when(jnp.logical_not(is_last))
+    def _():
+        bulk(0, last - 1).start()
+
+    @pl.when(is_inner)
+    def _():
+        edge(1).start()
+
+    @pl.when(jnp.logical_and(is_inner, jnp.logical_not(is_middle)))
+    def _():
+        for c in range(1, last):
+            bulk(1, c).start()
+
+    @pl.when(ends)
+    def _():
+        pl.semaphore_wait(row_sem.at[1], 1)
+        tile(1).start()
+        edge(1).start()
+        for c in range(last):
+            bulk(1, c).start()
 
     @pl.when(my_grp == 0)
     def _():
@@ -336,6 +437,17 @@
     for c in range(FIRST):
         finish_chunk(c)
 
+    onward = hop(passed, passed, (my_grp, my_aa - to_low), pass_send_sem, pass_recv_sem)
+    home = hop(passed, got.at[0, block, lines], ahead_id, pass_send_sem, recv_sem.at[0, last - 1])
+    arrived = pltpu.make_async_copy(passed, passed, pass_recv_sem)
+
+    @pl.when(is_middle)
+    def _():
+        arrived.wait()
+        onward.start()
+        for c in range(1, last):
+            bulk(1, c).start()
+
     for d in range(2):
         edge(d).wait_recv()
     for copy in smalls[3:]:
@@ -400,6 +512,16 @@
 
     for c in range(SECOND, last):
         finish_chunk(c)
+
+    @pl.when(is_low)
+    def _():
+        arrived.wait()
+        home.start()
+        home.wait_send()
+
+    @pl.when(is_middle)
+    def _():
+        onward.wait_send()
 
     pltpu.make_async_copy(parts_got, parts_got, part_send_sem).wait()
     for d in range(2):
@@ -448,6 +570,7 @@
             vmem((rows, width), jnp.int32),
             vmem((rows, width), jnp.int32),
             vmem((2, freqs, DIRS, width), F32),
+            vmem((chunks[last] - chunks[last - 1], DIRS, width), F32),
             vmem((freqs, 4, 8, width), F32),
             vmem((freqs, 4, 8, width), F32),
             vmem((8, width), F32),
@@ -470,6 +593,9 @@
             dma((2,)),
             dma,
             dma,
+            dma,
+            dma,
+            pltpu.SemaphoreType.REGULAR((2,)),
             pltpu.SemaphoreType.REGULAR,
             pltpu.SemaphoreType.REGULAR,
         ],

time: 40.6 us -> 40.1 us (0.988)
  Pallas kernels: 39.8 us -> 39.3 us
    pallas_call x1, Pallas kernels: 38.6 us -> 38.1 us  [on_device(): pl.pallas_call(functools.partial(kernel, chunks), out_shape=(vmem((freqs,...]
where the time goes in v5:
time: 40.1 us; the launch traced here: 39.9 us
  Pallas kernels  39.3 us (98%)
  between operations  0.64 us (2%)
    pallas_call x1, Pallas kernels, on_device(): pl.pallas_call(functools.partial(kernel, chunks), out_shape=(vmem((freqs,...  38.1 us
    pallas_call x1, Pallas kernels, on_device(): pl.pallas_call(pass_on, out_shape=results, in_specs=[inside] * 2, out_spe...  1.21 us

profile of v5, /device:TPU:1, one launch (start us, length us, event | category | flops | bytes accessed | tf_op | source)
XLA Modules:
  0.0 39.9 jit_solution(16692318228184712971)
XLA Ops:
  0.6 38.1 %shard_map.77 = (f32[50,64,128]{2,1,0:T(8,128)S(1)}, f32[3,256]{1,0:T(4,128)S(1)}) custom-call(f32[50,64,128]{2,1,0:T(8,128)} %bitcast.3, f32[2,128]{1,0:T(2,128)} %friction_hbm.1, f32[2,128]{1,0:T(2,128)} %wind_hbm.1, s32[128,128]{1,0:T(8,128)} %wet_hbm.1, s32[2,128]{1,0:T(2,128)} %bitcast.4, s32[2,128]{1,0:T(2,128)} %cell_hbm.1), custom_call_target="tpu_custom_call" | custom-call | tf_op jit(solution)/shard_map/pallas_call | solution.py:560
  38.7 1.2 %shard_map.78 = (f32[50,64,128]{2,1,0:T(8,128)}, f32[3,256]{1,0:T(4,128)}) custom-call(f32[50,64,128]{2,1,0:T(8,128)S(1)} %get-tuple-element.6.new, f32[3,256]{1,0:T(4,128)S(1)} %get-tuple-element.7.forcing), custom_call_target="tpu_custom_call" | custom-call | tf_op jit(solution)/shard_map/pallas_call | solution.py:613

commit v6 on v5

--- a/solution.py
+++ b/solution.py
@@ -12,8 +12,8 @@
 DIRS = 32
 COURANT = 0.7
 LOG2E = math.log2(math.e)
-CHUNKS = (0, 15, 30, 44, 47, 50)
-FIRST, SECOND = 1, 3
+CHUNKS = (0, 10, 28, 44, 47, 50)
+FIRST, SECOND = 1, 4
 PIECES = 4
 LIMIT = 60 * 1024 * 1024
 F32 = jnp.float32
@@ -179,6 +179,7 @@
 
     @pl.when(is_late)
     def _():
+        pl.semaphore_signal(row_sem.at[1], inc=1, device_id=row_ids[0], device_id_type=MESH)
         bulk(0, 0).start()
 
     @pl.when(is_last)
@@ -195,10 +196,6 @@
     def _():
         bulk(1, 0).start()
         pl.semaphore_signal(row_sem.at[0], inc=1, device_id=row_ids[1], device_id_type=MESH)
-
-    @pl.when(is_late)
-    def _():
-        pl.semaphore_signal(row_sem.at[1], inc=1, device_id=row_ids[0], device_id_type=MESH)
 
     for copy in smalls[:3] + loads + smalls[3:]:
         copy.start()

time: 40.1 us -> 39.8 us (level)
  no operation moved by 1% of the time
where the time goes in v6:
time: 39.8 us; the launch traced here: 39.6 us
  Pallas kernels  39 us (98%)
  between operations  0.64 us (2%)
    pallas_call x1, Pallas kernels, on_device(): pl.pallas_call(functools.partial(kernel, chunks), out_shape=(vmem((freqs,...  37.8 us
    pallas_call x1, Pallas kernels, on_device(): pl.pallas_call(pass_on, out_shape=results, in_specs=[inside] * 2, out_spe...  1.21 us

profile of v6, /device:TPU:1, one launch (start us, length us, event | category | flops | bytes accessed | tf_op | source)
XLA Modules:
  0.0 39.6 jit_solution(16386329212015046712)
XLA Ops:
  0.6 37.8 %shard_map.77 = (f32[50,64,128]{2,1,0:T(8,128)S(1)}, f32[3,256]{1,0:T(4,128)S(1)}) custom-call(f32[50,64,128]{2,1,0:T(8,128)} %bitcast.3, f32[2,128]{1,0:T(2,128)} %friction_hbm.1, f32[2,128]{1,0:T(2,128)} %wind_hbm.1, s32[128,128]{1,0:T(8,128)} %wet_hbm.1, s32[2,128]{1,0:T(2,128)} %bitcast.4, s32[2,128]{1,0:T(2,128)} %cell_hbm.1), custom_call_target="tpu_custom_call" | custom-call | tf_op jit(solution)/shard_map/pallas_call | solution.py:557
  38.4 1.2 %shard_map.78 = (f32[50,64,128]{2,1,0:T(8,128)}, f32[3,256]{1,0:T(4,128)}) custom-call(f32[50,64,128]{2,1,0:T(8,128)S(1)} %get-tuple-element.6.new, f32[3,256]{1,0:T(4,128)S(1)} %get-tuple-element.7.forcing), custom_call_target="tpu_custom_call" | custom-call | tf_op jit(solution)/shard_map/pallas_call | solution.py:610
